TPU v7x, 32 devices: a whole 2x2x4 slice. The times are simulated.
32 devices in a mesh: group: 2 (over y), dp: 8 (over z, x), tensor: 2 (over core).
Axes of the slice: x: 2, y: 2, z: 4, core: 2. Of those that a mesh axis runs over, the one named last changes fastest.
Arguments:
- queries: bfloat16 [2048, 8, 4096], P(('group', 'dp'), None, 'tensor'), parts along dimension 0, may hold values from -6 to 6
- key_value_pairs: bfloat16 [2048, 8, 1024], P(('group', 'dp'), None, 'tensor'), parts along dimension 0, may hold values from -6 to 6
- prompt_cache: bfloat16 [2048, 1024], P('group', 'tensor'), parts along dimension 0, may hold values from -6 to 6
- score_weight: bfloat16 [4096], P('tensor'), may hold values from -4 to 4
- old_values: float32 [2048, 8], P(('group', 'dp')), parts along dimension 0, may hold values from -6 to 6
- lengths: int32 [2048], P('group'), parts along dimension 0, may hold values from 1 to 8, as said below
- target_rank: int32 [2048], P('group'), parts along dimension 0, may hold values from 0 to 7, as said below
Outputs:
- attention: bfloat16 [2048, 8, 4096], P(('group', 'dp'), None, 'tensor'), parts along dimension 0
- score_delta: float32 [2048, 8], P(('group', 'dp')), parts along dimension 0
There are 2 independent parts, one for each index of `group`. A program takes and returns all parts, laid end to end along the dimension named above; an argument that names none is the same for every part. Nothing has to cross between parts.
Inputs may be any that keep to these rules, and one draw needn't show every extreme that they name: `lengths`: some response has exactly 8 tokens in every draw. `target_rank`: for every slot index t, the t-th responses of the 8 indices of dp go to 8 different indices, so every index receives one response for each slot index. Two indices of dp that send one another any responses send exactly 16.
All inputs are finite; a program needn't handle non-finite values.
Results may differ from a plain program's by a relative error of at most 0.0047.
Values may be sent and summed in bfloat16 or wider, within the bound.
A program may use at most 128 MiB of HBM per device.

v0:
```python
import jax
import jax.numpy as jnp
from jax import lax
from jax.sharding import PartitionSpec as P

HEAD_SIZE = 128


def attend_block(queries, key_value_pairs, prompt_cache, seq_lens):
    blocks, slot_len, feature_width = queries.shape
    pair_heads = key_value_pairs.shape[2] // (2 * HEAD_SIZE)
    head_total = feature_width // HEAD_SIZE
    groups = head_total // pair_heads
    score_scale = HEAD_SIZE ** (-0.5)
    prompt_len = prompt_cache.shape[0]
    query_split = queries.reshape(blocks, slot_len, pair_heads, groups, HEAD_SIZE)
    own_pairs = key_value_pairs.reshape(blocks, slot_len, pair_heads, 2, HEAD_SIZE)
    cache_pairs = prompt_cache.reshape(prompt_len, pair_heads, 2, HEAD_SIZE)
    prompt_scores = (
        jnp.einsum(
            "bshgd,phd->bshgp",
            query_split,
            cache_pairs[:, :, 0],
            preferred_element_type=jnp.float32,
        )
        * score_scale
    )
    own_scores = (
        jnp.einsum(
            "bshgd,bthd->bshgt",
            query_split,
            own_pairs[:, :, :, 0],
            preferred_element_type=jnp.float32,
        )
        * score_scale
    )
    position = jnp.arange(slot_len)
    causal = position[None, :] <= position[:, None]
    own_scores = jnp.where(causal[None, :, None, None, :], own_scores, -1e30)
    row_top = jnp.maximum(jnp.max(prompt_scores, -1), jnp.max(own_scores, -1))
    prompt_exp = jnp.exp(prompt_scores - row_top[..., None])
    own_exp = jnp.exp(own_scores - row_top[..., None])
    denominator = jnp.sum(prompt_exp, -1) + jnp.sum(own_exp, -1)
    prompt_probs = prompt_exp.astype(jnp.bfloat16)
    own_probs = own_exp.astype(jnp.bfloat16)
    weighted = jnp.einsum(
        "bshgp,phd->bshgd", prompt_probs, cache_pairs[:, :, 1], preferred_element_type=jnp.float32
    )
    weighted = weighted + jnp.einsum(
        "bshgt,bthd->bshgd", own_probs, own_pairs[:, :, :, 1], preferred_element_type=jnp.float32
    )
    result = weighted / denominator[..., None]
    live_rows = position[None, :] < seq_lens[:, None]
    result = jnp.where(live_rows[:, :, None, None, None], result, 0.0)
    return result.reshape(blocks, slot_len, feature_width).astype(jnp.bfloat16)


def attend_all(queries, key_value_pairs, prompt_cache, seq_lens):
    seq_count, slot_len, feature_width = queries.shape
    block_sequences = min(seq_count, max(1, 512 // slot_len))
    step_count = seq_count // block_sequences

    def one_block(pieces):
        return attend_block(pieces[0], pieces[1], prompt_cache, pieces[2])

    result = lax.map(
        one_block,
        (
            queries.reshape(step_count, block_sequences, slot_len, feature_width),
            key_value_pairs.reshape(
                step_count, block_sequences, slot_len, key_value_pairs.shape[2]
            ),
            seq_lens.reshape(step_count, block_sequences),
        ),
    )
    return result.reshape(seq_count, slot_len, feature_width)


def head_scores(attention, score_weight):
    seq_count, slot_len, feature_width = attention.shape
    partial_sum = jnp.dot(
        attention.reshape(seq_count * slot_len, feature_width),
        score_weight,
        preferred_element_type=jnp.float32,
    ).reshape(seq_count, slot_len)
    return lax.psum(partial_sum, "tensor")


def pack_rows(values, source, present):
    taken_rows = jnp.take(values, source, axis=0)
    mask_shape = (present.shape[0],) + (1,) * (values.ndim - 1)
    return jnp.where(present.reshape(mask_shape), taken_rows, jnp.zeros_like(taken_rows))


def shards(queries, key_value_pairs, prompt_cache, score_weight, old_values, lengths, target_rank):
    my_rank = lax.axis_index("dp")
    rank_count = lax.axis_size("dp")
    seq_count, slot_len, feature_width = queries.shape
    capacity = max(2, seq_count // rank_count)
    buffer_slots = rank_count * capacity
    target_plan = target_rank.reshape(rank_count, seq_count)
    all_lens = lengths.reshape(rank_count, seq_count)
    my_targets = lax.dynamic_index_in_dim(target_plan, my_rank, 0, keepdims=False)
    my_lens = lax.dynamic_index_in_dim(all_lens, my_rank, 0, keepdims=False)
    slot_order = jnp.arange(seq_count, dtype=jnp.int32)
    earlier = (my_targets[:, None] == my_targets[None, :]) & (
        slot_order[None, :] < slot_order[:, None]
    )
    send_pos = my_targets * capacity + jnp.sum(earlier, axis=1)
    buffer_index = jnp.arange(buffer_slots, dtype=jnp.int32)
    send_match = send_pos[None, :] == buffer_index[:, None]
    send_source = jnp.sum(jnp.where(send_match, slot_order[None, :], 0), axis=1)
    send_present = jnp.any(send_match, axis=1)
    arriving = target_plan == my_rank
    arrive_rank = jnp.cumsum(arriving.astype(jnp.int32), axis=1) - 1
    sources = jnp.arange(rank_count, dtype=jnp.int32)
    recv_pos = jnp.sum(jnp.where(arriving, sources[:, None] * capacity + arrive_rank, 0), axis=0)
    local_rows = attend_all(queries, key_value_pairs, prompt_cache, my_lens)
    new_values = head_scores(local_rows, score_weight)
    moved_rows = lax.all_to_all(
        pack_rows(local_rows, send_source, send_present),
        "dp",
        split_axis=0,
        concat_axis=0,
        tiled=True,
    )
    attention = jnp.take(moved_rows, recv_pos, axis=0)
    position = jnp.arange(slot_len)
    live_rows = position[None, :] < my_lens[:, None]
    score_delta = jnp.where(live_rows, new_values - old_values, 0.0)
    return (attention, score_delta)


def solution(mesh):
    placed = (
        P(("group", "dp"), None, "tensor"),
        P(("group", "dp"), None, "tensor"),
        P("group", "tensor"),
        P("tensor"),
        P(("group", "dp"), None),
        P("group"),
        P("group"),
    )
    return jax.shard_map(
        shards,
        mesh=mesh,
        in_specs=placed,
        out_specs=(P(("group", "dp"), None, "tensor"), P(("group", "dp"), None)),
        check_vma=False,
    )
```

profile of v0, /device:TPU:0, one launch (start us, length us, event | category | flops | bytes accessed | tf_op | source)
XLA Modules:
  0.0 275.9 jit_solution(5589997801125570534)
XLA Ops:
  0.6 0.7 fusion.25
  1.5 0.7 fusion.24
  2.3 0.6 compare_select_fusion.1
  2.9 0.6 compare_and_fusion.1
  3.5 0.7 fusion.22
  4.2 1.3 fusion.26
  5.6 2.3 copy.74
  7.8 148.7 %while.10 = (s32[]{:T(128)}, bf16[2,64,8,2048]{3,2,1,0:T(8,128)(2,1)}, s32[2,64]{1,0:T(2,128)S(1)}, bf16[2,64,8,2048]{3,2,1,0:T(8,128)(2,1)}, bf16[1024,512]{0,1...) while((s32[]{:T(128)}, bf16[2,64,8,2048]{3,2,1,0:T(8,128)(2,1)}, s32[2,64]{1,0:T(2,128)S(1)}, ...), condition=%wide.region_7.8_spmd, body=%wide.region_2.7_spmd.sunk | while | flops 4400333312 | bytes 148579952 | solution.py:66
  7.8 1.1 constant_dynamic-slice_fusion.5
  8.9 1.9 dynamic-slice_bitcast_fusion.2
  10.9 11.2 %fusion.49 = f32[64,2,8,8,8]{4,2,3,1,0:T(8,128)} fusion(bf16[64,8,2,2,128]{4,1,3,2,0:T(8,128)(2,1)S(1)} %bitcast.136, bf16[64,8,16,128]{3,1,2,0:T(8,128)(2,1)S(1)} %dynamic-slice_bitcast_fusion.2), kind=kOutput, calls=%fused_computation.15.clone.1 | convolution fusion | flops 16777216 | bytes 2621440 | tf_op jit(solution)/shard_map/while/body/eval_jaxpr/bshgd,bthd->bshgt/dot_general | solution.py:29
  22.1 3.7 %copy.117 = f32[64,2,8,8,8]{0,2,4,1,3:T(8,128)S(1)} copy(f32[64,2,8,8,8]{4,2,3,1,0:T(8,128)} %fusion.49) | data formatting | bytes 524288 | tf_op jit(solution)/shard_map/while/body/eval_jaxpr/bshgd,bthd->bshgt/dot_general | solution.py:29
  25.8 14.2 %bitcast_reduce_fusion.2 = (f32[64,8,2,8]{3,1,0,2:T(8,128)S(1)}, f32[2,64,8,8,1024]{4,3,2,1,0:T(8,128)}) fusion(bf16[1024,2,2,128]{0,3,2,1:T(8,128)(2,1)} %bitcast.141, bf16[64,8,16,128]{3,1,2,0:T(8,128)(2,1)S(1)} %dynamic-slice_bitcast_fusion.2), kind=kOutput, calls=%fused_computation.3.clone.1 | convolution fusion | flops 2164252672 | bytes 36208640 | tf_op jit(solution)/shard_map/while/body/eval_jaxpr/bshgd,phd->bshgp/dot_general | solution.py:20
  40.3 0.3 fusion.50
  40.6 0.3 fusion.51
  40.9 3.2 %copy.119 = bf16[64,8,2,8,8]{4,3,1,0,2:T(8,128)(2,1)S(1)} copy(bf16[64,8,2,8,8]{0,4,3,2,1:T(8,128)(2,1)S(1)} %get-tuple-element.128) | data formatting | bytes 262144 | tf_op jit(solution)/shard_map/while/body/eval_jaxpr/convert_element_type | solution.py:45
  44.1 2.7 fusion.52
  47.1 14.3 %fusion.53 = f32[64,8,2,8]{3,1,0,2:T(8,128)S(1)} fusion(f32[2,64,8,8,1024]{4,3,2,1,0:T(8,128)} %get-tuple-element.129, f32[64,8,2,8]{3,1,0,2:T(8,128)S(1)} %copy.120), kind=kLoop, calls=%fused_computation.5.clone.1 | loop fusion | flops 25157632 | bytes 33619968 | tf_op jit(solution)/shard_map/while/body/eval_jaxpr/reduce_sum | solution.py:43
  61.4 0.2 copy.121
  61.8 14.3 %fusion.55 = bf16[64,8,2,8,128]{4,3,1,0,2:T(8,128)(2,1)S(1)} fusion(f32[64,2,128,8,8]{2,4,3,0,1:T(8,128)} %fusion.52, f32[2,64,8,8,1024]{4,3,2,1,0:T(8,128)} %get-tuple-element.129, f32[64,8,2,8]{3,1,0,2:T(8,128)S(1)} %copy.120, f32[64,8,2,8]{3,1,0,2:T(8,128)S(1)} %add.81, pred[64,8]{1,0:T(8,128)(4,1)S(1)} %iota_compare_fusion.8, ...), kind=kOutput, calls=%fused_computation.13.clone.1 | convolution fusion | flops 2176843776 | bytes 41426944 | tf_op jit(solution)/shard_map/while/body/eval_jaxpr/bshgp,phd->bshgd/dot_general | solution.py:46
  76.2 1.7 copy.122
  77.9 2.8 %convert_element_type.40 = bf16[1,64,8,2048]{3,2,1,0:T(8,128)(2,1)S(1)} reshape(bf16[64,8,2,8,128]{4,3,2,1,0:T(8,128)(2,1)} %copy.122) | data formatting | bytes 4194304 | tf_op jit(solution)/shard_map/while/body/eval_jaxpr/convert_element_type | solution.py:55
  80.7 1.5 constant_dynamic-update-slice_fusion.2
  82.2 1.1 constant_dynamic-slice_fusion.5
  83.3 1.9 dynamic-slice_bitcast_fusion.2
  85.2 11.2 %fusion.49 = f32[64,2,8,8,8]{4,2,3,1,0:T(8,128)} fusion(bf16[64,8,2,2,128]{4,1,3,2,0:T(8,128)(2,1)S(1)} %bitcast.136, bf16[64,8,16,128]{3,1,2,0:T(8,128)(2,1)S(1)} %dynamic-slice_bitcast_fusion.2), kind=kOutput, calls=%fused_computation.15.clone.1 | convolution fusion | flops 16777216 | bytes 2621440 | tf_op jit(solution)/shard_map/while/body/eval_jaxpr/bshgd,bthd->bshgt/dot_general | solution.py:29
  96.5 3.7 %copy.117 = f32[64,2,8,8,8]{0,2,4,1,3:T(8,128)S(1)} copy(f32[64,2,8,8,8]{4,2,3,1,0:T(8,128)} %fusion.49) | data formatting | bytes 524288 | tf_op jit(solution)/shard_map/while/body/eval_jaxpr/bshgd,bthd->bshgt/dot_general | solution.py:29
  100.2 14.2 %bitcast_reduce_fusion.2 = (f32[64,8,2,8]{3,1,0,2:T(8,128)S(1)}, f32[2,64,8,8,1024]{4,3,2,1,0:T(8,128)}) fusion(bf16[1024,2,2,128]{0,3,2,1:T(8,128)(2,1)} %bitcast.141, bf16[64,8,16,128]{3,1,2,0:T(8,128)(2,1)S(1)} %dynamic-slice_bitcast_fusion.2), kind=kOutput, calls=%fused_computation.3.clone.1 | convolution fusion | flops 2164252672 | bytes 36208640 | tf_op jit(solution)/shard_map/while/body/eval_jaxpr/bshgd,phd->bshgp/dot_general | solution.py:20
  114.6 0.3 fusion.50
  114.9 0.3 fusion.51
  115.3 3.2 %copy.119 = bf16[64,8,2,8,8]{4,3,1,0,2:T(8,128)(2,1)S(1)} copy(bf16[64,8,2,8,8]{0,4,3,2,1:T(8,128)(2,1)S(1)} %get-tuple-element.128) | data formatting | bytes 262144 | tf_op jit(solution)/shard_map/while/body/eval_jaxpr/convert_element_type | solution.py:45
  118.5 2.7 fusion.52
  121.5 14.3 %fusion.53 = f32[64,8,2,8]{3,1,0,2:T(8,128)S(1)} fusion(f32[2,64,8,8,1024]{4,3,2,1,0:T(8,128)} %get-tuple-element.129, f32[64,8,2,8]{3,1,0,2:T(8,128)S(1)} %copy.120), kind=kLoop, calls=%fused_computation.5.clone.1 | loop fusion | flops 25157632 | bytes 33619968 | tf_op jit(solution)/shard_map/while/body/eval_jaxpr/reduce_sum | solution.py:43
  135.8 0.2 copy.121
  136.2 14.3 %fusion.55 = bf16[64,8,2,8,128]{4,3,1,0,2:T(8,128)(2,1)S(1)} fusion(f32[64,2,128,8,8]{2,4,3,0,1:T(8,128)} %fusion.52, f32[2,64,8,8,1024]{4,3,2,1,0:T(8,128)} %get-tuple-element.129, f32[64,8,2,8]{3,1,0,2:T(8,128)S(1)} %copy.120, f32[64,8,2,8]{3,1,0,2:T(8,128)S(1)} %add.81, pred[64,8]{1,0:T(8,128)(4,1)S(1)} %iota_compare_fusion.8, ...), kind=kOutput, calls=%fused_computation.13.clone.1 | convolution fusion | flops 2176843776 | bytes 41426944 | tf_op jit(solution)/shard_map/while/body/eval_jaxpr/bshgp,phd->bshgd/dot_general | solution.py:46
  150.5 1.7 copy.122
  152.2 2.8 %convert_element_type.40 = bf16[1,64,8,2048]{3,2,1,0:T(8,128)(2,1)S(1)} reshape(bf16[64,8,2,8,128]{4,3,2,1,0:T(8,128)(2,1)} %copy.122) | data formatting | bytes 4194304 | tf_op jit(solution)/shard_map/while/body/eval_jaxpr/convert_element_type | solution.py:55
  155.1 1.5 constant_dynamic-update-slice_fusion.2
  156.6 5.0 %gather_fusion = bf16[128,8,2048]{2,1,0:T(8,128)(2,1)} fusion(bf16[128,8,2048]{2,1,0:T(8,128)(2,1)} %bitcast.139, s32[1024]{0:T(1024)S(1)} %pad_clamp_fusion.1), kind=kCustom, calls=%fused_computation.clone | custom fusion | bytes 8389120 | tf_op jit(solution)/shard_map/jit(_take)/gather | solution.py:90
  161.6 4.1 %select_select_fusion = bf16[128,8,2048]{2,1,0:T(8,128)(2,1)} fusion(bf16[128,8,2048]{2,1,0:T(8,128)(2,1)} %gather_fusion, pred[128]{0:T(512)(128)(4,1)S(1)} %copy-done.7, pred[128]{0:T(512)(128)(4,1)S(1)} %copy-done.8), kind=kLoop, calls=%fused_computation.37 | loop fusion | flops 4194304 | bytes 8388864 | tf_op jit(solution)/shard_map/jit(_where)/select_n | solution.py:92
  165.6 7.4 %all-to-all-start = ((bf16[128,8,2048]{2,1,0:T(8,128)(2,1)}), bf16[128,8,2048]{2,1,0:T(8,128)(2,1)}, u32[]{:S(2)}, u32[]{:S(2)}) async-start(bf16[128,8,2048]{2,1,0:T(8,128)(2,1)} %select_select_fusion), calls=%async_computation | async-start | bytes 8388608 | tf_op jit(solution)/shard_map/all_to_all | solution.py:120
  173.1 0.3 reduce_window_sum.11
  173.3 11.5 %fusion.29 = f32[1,128,8]{2,0,1:T(1,128)S(1)} fusion(bf16[128,8,2048]{2,1,0:T(8,128)(2,1)} %bitcast.140, bf16[2048,1,1]{0,1,2:T(2,128)(2,1)S(1)} %reshape.145), kind=kOutput, calls=%fused_computation.64 | convolution fusion | flops 4194304 | bytes 4202496 | tf_op jit(solution)/shard_map/dot_general | solution.py:81
  184.9 2.5 psum.7
  187.5 0.6 subtract_select_fusion
  188.1 78.2 %all-to-all-done = bf16[128,8,2048]{2,1,0:T(8,128)(2,1)} async-done(((bf16[128,8,2048]{2,1,0:T(8,128)(2,1)}), bf16[128,8,2048]{2,1,0:T(8,128)(2,1)}, u32[]{:S(2)}, u32[]{:S(2)}) %all-to-all-start) | async-done | bytes 4194336 | tf_op jit(solution)/shard_map/all_to_all | solution.py:120
  266.3 5.0 %gather_fusion.1 = bf16[128,8,2048]{2,1,0:T(8,128)(2,1)} fusion(bf16[128,8,2048]{2,1,0:T(8,128)(2,1)} %all-to-all-done, s32[1024]{0:T(1024)S(1)} %pad_clamp_fusion), kind=kCustom, calls=%fused_computation.1.clone | custom fusion | bytes 8389120 | tf_op jit(solution)/shard_map/jit(_take)/gather | solution.py:127
  271.3 4.6 %broadcast_select_fusion = bf16[128,8,2048]{2,1,0:T(8,128)(2,1)} fusion(bf16[128,8,2048]{2,1,0:T(8,128)(2,1)} %gather_fusion.1, pred[128]{0:T(512)(128)(4,1)S(1)} %compare_and_fusion), kind=kLoop, calls=%fused_computation.38 | loop fusion | flops 2097152 | bytes 8388736 | tf_op jit(solution)/shard_map/jit(_take)/select_n | solution.py:127
  (53 shorter events, 1.8 us)
Async XLA Ops:
  7.8 148.7 %copy-start.9 = (s32[128]{0:T(128)S(1)}, s32[128]{0:T(128)}, u32[]{:S(2)}) copy-start(s32[128]{0:T(128)} %compare_select_fusion.1) | copy-start | bytes 1540
  8.9 1.9 copy-start
  40.1 4.1 %copy-start.1 = (bf16[1,64,8,512]{3,2,1,0:T(8,128)(2,1)S(1)}, bf16[1,64,8,512]{3,2,1,0:T(8,128)(2,1)}, u32[]{:S(2)}) copy-start(bf16[1,64,8,512]{3,2,1,0:T(8,128)(2,1)} %copy-done) | copy-start | bytes 1572868 | tf_op jit(solution)/shard_map/while
  47.1 14.7 %copy-start.2 = (bf16[1024,512]{0,1:T(8,128)(2,1)S(1)}, bf16[1024,512]{0,1:T(8,128)(2,1)}, u32[]{:S(2)}) copy-start(bf16[1024,512]{0,1:T(8,128)(2,1)} %get-tuple-element.149) | copy-start | bytes 3145732 | tf_op jit(solution)/shard_map/while
  83.3 1.9 copy-start
  114.4 4.1 %copy-start.1 = (bf16[1,64,8,512]{3,2,1,0:T(8,128)(2,1)S(1)}, bf16[1,64,8,512]{3,2,1,0:T(8,128)(2,1)}, u32[]{:S(2)}) copy-start(bf16[1,64,8,512]{3,2,1,0:T(8,128)(2,1)} %copy-done) | copy-start | bytes 1572868 | tf_op jit(solution)/shard_map/while
  121.5 14.7 %copy-start.2 = (bf16[1024,512]{0,1:T(8,128)(2,1)S(1)}, bf16[1024,512]{0,1:T(8,128)(2,1)}, u32[]{:S(2)}) copy-start(bf16[1024,512]{0,1:T(8,128)(2,1)} %get-tuple-element.149) | copy-start | bytes 3145732 | tf_op jit(solution)/shard_map/while
  156.6 5.0 %copy-start.7 = (pred[128]{0:T(512)(128)(4,1)S(1)}, pred[128]{0:T(512)(128)(4,1)}, u32[]{:S(2)}) copy-start(pred[128]{0:T(512)(128)(4,1)} %compare_and_fusion.1) | copy-start | bytes 388
  156.6 5.0 %copy-start.8 = (pred[128]{0:T(512)(128)(4,1)S(1)}, pred[128]{0:T(512)(128)(4,1)}, u32[]{:S(2)}) copy-start(pred[128]{0:T(512)(128)(4,1)} %fusion.22) | copy-start | bytes 388
  165.6 7.4 %copy-start.3 = (s32[1024]{0:T(1024)S(1)}, s32[1024]{0:T(1024)}, u32[]{:S(2)}) copy-start(s32[1024]{0:T(1024)} %param.17) | copy-start | bytes 12292
  165.6 7.7 %copy-start.4 = (bf16[2048]{0:T(1024)(128)(2,1)S(1)}, bf16[2048]{0:T(1024)(128)(2,1)}, u32[]{:S(2)}) copy-start(bf16[2048]{0:T(1024)(128)(2,1)} %param.14) | copy-start | bytes 12292
  165.6 100.7 %all-to-all-start = ((bf16[128,8,2048]{2,1,0:T(8,128)(2,1)}), bf16[128,8,2048]{2,1,0:T(8,128)(2,1)}, u32[]{:S(2)}, u32[]{:S(2)}) async-start(bf16[128,8,2048]{2,1,0:T(8,128)(2,1)} %select_select_fusion), calls=%async_computation | async-start | bytes 8388608 | tf_op jit(solution)/shard_map/all_to_all | solution.py:120
  173.0 14.5 %copy-start.5 = (f32[128,8]{0,1:T(8,128)S(1)}, f32[128,8]{0,1:T(8,128)}, u32[]{:S(2)}) copy-start(f32[128,8]{0,1:T(8,128)} %param.15) | copy-start | bytes 12292
  173.0 14.5 %copy-start.6 = (s32[128]{0:T(128)S(1)}, s32[128]{0:T(128)}, u32[]{:S(2)}) copy-start(s32[128]{0:T(128)} %get-tuple-element.84) | copy-start | bytes 1540
where the time goes:
time: 277 us; the launch traced here: 276 us
  matrix products  96.5 us (35%)
  waiting for transfers between devices  78.2 us (28%)
  local copies, waits for them, and re-layouts  47.8 us (17%)
  other arithmetic  42.6 us (15%)
  starting transfers between devices  7.39 us (3%)
    all_to_all x1, waiting for transfers between devices, shards(): lax.all_to_all(pack_rows(local_rows, send_source, send_present), 'dp', sp...  78.2 us
    reduce_sum x4, other arithmetic, attend_block(): denominator = jnp.sum(prompt_exp, -1) + jnp.sum(own_exp, -1)  29.2 us
    dot_general x2, matrix products, attend_block(): jnp.einsum('bshgp,phd->bshgd', prompt_probs, cache_pairs[:, :, 1], prefer...  28.7 us
    dot_general x2, matrix products, attend_block(): jnp.einsum('bshgd,phd->bshgp', query_split, cache_pairs[:, :, 0], preferr...  28.5 us
    dot_general x2, matrix products, attend_block(): jnp.einsum('bshgd,bthd->bshgt', query_split, own_pairs[:, :, :, 0], prefe...  22.5 us
    dot_general x1, matrix products, head_scores(): jnp.dot(attention.reshape(seq_count * slot_len, feature_width), score_wei...  11.5 us
    convert_element_type x4, local copies, waits for them, and re-layouts, attend_block(): return result.reshape(blocks, slot_len, feature_width).astype(jnp.bfloat16)  9.13 us
    dot_general x2, local copies, waits for them, and re-layouts, attend_block(): jnp.einsum('bshgd,bthd->bshgt', query_split, own_pairs[:, :, :, 0], prefe...  7.47 us
  transfers between devices with their start and end apart: 1, of which 1 were waited for; matrix products, arithmetic and copies ran while one was open for 5% of the time, Pallas kernels for 0%

commit v1 on v0

v1 whole, which is shorter than its diff:
```python
import functools
import math

import jax
import jax.numpy as jnp
from jax import lax
from jax.experimental import pallas as pl
from jax.experimental.pallas import tpu as pltpu
from jax.sharding import PartitionSpec as P

HEAD = 128
BLOCK = 16
STACK = 4
MESH = pl.DeviceIdType.MESH
NEG = -1e30


def xor(a, b, n):
    total, bit = 0, 1
    while bit < n:
        total = total + ((a // bit + b // bit) % 2) * bit
        bit *= 2
    return total


def score_kernel(
    n, rows, slot_len,
    order_ref, lo_ref, hi_ref, tok_ref, q_ref, kv_ref, prompt_ref, w_ref, old_ref,
    recv_ref, delta_ref,
    keys, vals, qf, kvf, qc, send, nv_send, nv_recv,
    send_sem, recv_sem, self_sem, nv_send_sem, nv_recv_sem,
):
    me = lax.axis_index("dp")
    core = lax.axis_index("tensor")
    slots = q_ref.shape[0]
    blocks = slots // BLOCK
    per_block = n // blocks
    part = rows // per_block
    tokens = BLOCK * slot_len
    prompt_len = prompt_ref.shape[0]
    pair_heads = prompt_ref.shape[1] // (2 * HEAD)
    groups = q_ref.shape[2] // HEAD // pair_heads
    scale = HEAD ** -0.5 * math.log2(math.e)

    barrier = pltpu.get_barrier_semaphore()

    def greet(m, _):
        pl.semaphore_signal(
            barrier, inc=1, device_id={"dp": xor(me, m, n)}, device_id_type=MESH
        )
        return _

    lax.fori_loop(1, n, greet, 0)
    pl.semaphore_signal(barrier, inc=1, device_id={"tensor": 1 - core}, device_id_type=MESH)

    def put_keys(g, at, size, k, v):
        scaled = k.astype(jnp.float32) * scale
        high = scaled.astype(jnp.bfloat16)
        low = (scaled - high.astype(jnp.float32)).astype(jnp.bfloat16)
        keys[g, pl.ds(at, size), :HEAD] = high
        keys[g, pl.ds(at, size), HEAD:] = low
        vals[g, pl.ds(at, size), :HEAD] = v

    vals[:, :, HEAD:] = jnp.ones_like(vals[:, :, HEAD:])
    for g in range(pair_heads):
        col = g * 2 * HEAD
        put_keys(g, 0, prompt_len, prompt_ref[:, col : col + HEAD],
                 prompt_ref[:, col + HEAD : col + 2 * HEAD])
    nv_send[...] = jnp.zeros_like(nv_send)
    pl.semaphore_wait(barrier, n)

    def outgoing(k):
        block, g = k // per_block, k % per_block
        return pltpu.make_async_remote_copy(
            src_ref=send.at[block, pl.ds(g * part, part)],
            dst_ref=recv_ref.at[k],
            send_sem=send_sem.at[k],
            recv_sem=recv_sem.at[k],
            device_id={"dp": xor(me, n - 1 - k, n)},
            device_id_type=MESH,
        )

    def one_block(j, _):
        for i in range(BLOCK):
            slot = order_ref[j * BLOCK + i]
            qf[pl.ds(i * slot_len, slot_len), :] = q_ref[slot].astype(jnp.float32)
            kvf[pl.ds(i * slot_len, slot_len), :] = kv_ref[slot].astype(jnp.float32)
        row = lax.broadcasted_iota(jnp.int32, (rows, tokens), 0)
        lo, hi = lo_ref[j], hi_ref[j]
        pick = jnp.where((lo == row) & (lo < hi), 1.0, 0.0).astype(jnp.bfloat16)
        qc[...] = jnp.dot(
            pick, qf[...].astype(jnp.bfloat16), preferred_element_type=jnp.float32
        ).astype(jnp.bfloat16)
        bias = jnp.where((lo <= row) & (row < hi), 0.0, NEG)
        bias = jnp.concatenate([bias] * STACK, axis=0)
        for g in range(pair_heads):
            col = g * 2 * HEAD
            put_keys(g, prompt_len, tokens, kvf[:, col : col + HEAD],
                     kvf[:, col + HEAD : col + 2 * HEAD].astype(jnp.bfloat16))

        def heads(step, nv):
            g = step // (groups // STACK)
            base = step * STACK * HEAD
            cols = [pl.ds(pl.multiple_of(base + h * HEAD, HEAD), HEAD) for h in range(STACK)]
            q = jnp.concatenate([qc[:, c] for c in cols], axis=0)
            q = jnp.concatenate([q, q], axis=1)
            s = lax.dot_general(
                q, keys[g], (((1,), (1,)), ((), ())), preferred_element_type=jnp.float32
            )
            sp = s[:, :prompt_len]
            so = s[:, prompt_len:] + bias
            top = jnp.maximum(
                jnp.max(sp, axis=1, keepdims=True), jnp.max(so, axis=1, keepdims=True)
            )
            probs = jnp.concatenate(
                [jnp.exp2(sp - top).astype(jnp.bfloat16), jnp.exp2(so - top).astype(jnp.bfloat16)],
                axis=1,
            )
            o = jnp.dot(probs, vals[g], preferred_element_type=jnp.float32)
            r = (o[:, :HEAD] / o[:, HEAD:]).astype(jnp.bfloat16)
            for h, c in enumerate(cols):
                piece = r[h * rows : (h + 1) * rows]
                send[j, :, c] = piece
                nv = nv + piece.astype(jnp.float32) * w_ref[:, c].astype(jnp.float32)
            return nv

        nv = lax.fori_loop(
            0, pair_heads * groups // STACK, heads, jnp.zeros((rows, HEAD), jnp.float32)
        )
        nv = jnp.sum(nv, axis=1, keepdims=True)
        wide = lax.broadcasted_iota(jnp.int32, (rows, slots * slot_len), 0) + j * rows
        nv_send[...] += jnp.sum(jnp.where(tok_ref[...] == wide, nv, 0.0), axis=0, keepdims=True)

        def start(g, _):
            outgoing(j * per_block + g).start()
            return _

        lax.fori_loop(0, jnp.where(j == blocks - 1, per_block - 1, per_block), start, 0)
        return _

    lax.fori_loop(0, blocks, one_block, 0)

    own = pltpu.make_async_copy(
        send.at[blocks - 1, pl.ds((per_block - 1) * part, part)], recv_ref.at[n - 1], self_sem
    )
    own.start()
    trade = pltpu.make_async_remote_copy(
        src_ref=nv_send, dst_ref=nv_recv, send_sem=nv_send_sem, recv_sem=nv_recv_sem,
        device_id={"tensor": 1 - core}, device_id_type=MESH,
    )
    trade.start()
    trade.wait()
    delta_ref[...] = jnp.where(
        tok_ref[...] >= 0, nv_send[...] + nv_recv[...] - old_ref[...], 0.0
    )
    own.wait()

    def finish(k, _):
        outgoing(k).wait()
        return _

    lax.fori_loop(0, n - 1, finish, 0)


def place_kernel(rows, slot_len, order_ref, lo_ref, hi_ref, recv_ref, out_ref):
    tokens = BLOCK * slot_len
    blocks = out_ref.shape[0] // BLOCK

    def one_block(j, _):
        row = lax.broadcasted_iota(jnp.int32, (rows, tokens), 0)
        lo, hi = lo_ref[j], hi_ref[j]
        pick = jnp.where((lo == row) & (lo < hi), 1.0, 0.0).astype(jnp.bfloat16)
        full = lax.dot_general(
            pick, recv_ref[j], (((0,), (0,)), ((), ())), preferred_element_type=jnp.float32
        )
        for i in range(BLOCK):
            out_ref[order_ref[j * BLOCK + i]] = full[
                i * slot_len : (i + 1) * slot_len
            ].astype(jnp.bfloat16)
        return _

    lax.fori_loop(0, blocks, one_block, 0)


def plan(partner, lens, me, n, rows, slot_len):
    slots = lens.shape[0]
    cap = slots // n
    per_block = BLOCK // cap
    slot = jnp.arange(slots, dtype=jnp.int32)
    earlier = (partner[:, None] == partner[None, :]) & (slot[None, :] < slot[:, None])
    rank = jnp.sum(earlier.astype(jnp.int32), axis=1)
    before = jnp.sum(jnp.where(earlier, lens[None, :], 0), axis=1)
    k = n - 1 - (partner ^ me)
    at = k * cap + rank
    first = (k % per_block) * (rows // per_block) + before
    match = at[None, :] == slot[:, None]

    def sort(x):
        return jnp.sum(jnp.where(match, x[None, :], 0), axis=1)

    position = jnp.arange(slot_len, dtype=jnp.int32)
    start = sort(first)
    lo = start[:, None] + position[None, :]
    hi = jnp.broadcast_to((start + sort(lens))[:, None], lo.shape)
    shape = (slots // BLOCK, 1, BLOCK * slot_len)
    token = jnp.where(
        position[None, :] < lens[:, None],
        ((k // per_block) * rows + first)[:, None] + position[None, :],
        -1,
    )
    return sort(slot), lo.reshape(shape), hi.reshape(shape), token.reshape(1, slots * slot_len)


def shards(queries, key_value_pairs, prompt_cache, score_weight, old_values, lengths, target_rank):
    me = lax.axis_index("dp").astype(jnp.int32)
    n = lax.axis_size("dp")
    slots, slot_len, width = queries.shape
    pair_heads = prompt_cache.shape[1] // (2 * HEAD)
    prompt_len = prompt_cache.shape[0]
    blocks = slots // BLOCK
    tokens = BLOCK * slot_len
    rows = tokens
    targets = target_rank.reshape(n, slots)
    lens = lengths.reshape(n, slots)
    my_targets = lax.dynamic_index_in_dim(targets, me, 0, keepdims=False)
    my_lens = lax.dynamic_index_in_dim(lens, me, 0, keepdims=False)
    arriving = targets == me
    ranks = jnp.arange(n, dtype=jnp.int32)
    source = jnp.sum(jnp.where(arriving, ranks[:, None], 0), axis=0)
    source_lens = jnp.sum(jnp.where(arriving, lens, 0), axis=0)
    order, lo, hi, token = plan(my_targets, my_lens, me, n, rows, slot_len)
    in_order, in_lo, in_hi, _ = plan(source, source_lens, me, n, rows, slot_len)

    smem = pl.BlockSpec(memory_space=pltpu.SMEM)
    vmem = pl.BlockSpec(memory_space=pltpu.VMEM)
    part = rows * blocks // n
    recv, delta = pl.pallas_call(
        functools.partial(score_kernel, n, rows, slot_len),
        out_shape=(
            jax.ShapeDtypeStruct((n, part, width), jnp.bfloat16),
            jax.ShapeDtypeStruct((1, slots * slot_len), jnp.float32),
        ),
        in_specs=[smem] + [vmem] * 8,
        out_specs=(pl.BlockSpec(memory_space=pl.ANY), vmem),
        scratch_shapes=[
            pltpu.VMEM((pair_heads, prompt_len + tokens, 2 * HEAD), jnp.bfloat16),
            pltpu.VMEM((pair_heads, prompt_len + tokens, 2 * HEAD), jnp.bfloat16),
            pltpu.VMEM((tokens, width), jnp.float32),
            pltpu.VMEM((tokens, prompt_cache.shape[1]), jnp.float32),
            pltpu.VMEM((rows, width), jnp.bfloat16),
            pltpu.VMEM((blocks, rows, width), jnp.bfloat16),
            pltpu.VMEM((1, slots * slot_len), jnp.float32),
            pltpu.VMEM((1, slots * slot_len), jnp.float32),
            pltpu.SemaphoreType.DMA((n,)),
            pltpu.SemaphoreType.DMA((n,)),
            pltpu.SemaphoreType.DMA,
            pltpu.SemaphoreType.DMA,
            pltpu.SemaphoreType.DMA,
        ],
        compiler_params=pltpu.CompilerParams(
            collective_id=0, has_side_effects=True, vmem_limit_bytes=48 * 2**20
        ),
    )(order, lo, hi, token, queries, key_value_pairs, prompt_cache,
      score_weight.reshape(1, width), old_values.reshape(1, slots * slot_len))

    attention = pl.pallas_call(
        functools.partial(place_kernel, rows, slot_len),
        out_shape=jax.ShapeDtypeStruct((slots, slot_len, width), jnp.bfloat16),
        in_specs=[smem, vmem, vmem, vmem],
        out_specs=vmem,
        compiler_params=pltpu.CompilerParams(vmem_limit_bytes=48 * 2**20),
    )(in_order, in_lo, in_hi, recv.reshape(blocks, rows, width))
    return attention, delta.reshape(slots, slot_len)


def solution(mesh):
    placed = (
        P(("group", "dp"), None, "tensor"),
        P(("group", "dp"), None, "tensor"),
        P("group", "tensor"),
        P("tensor"),
        P(("group", "dp"), None),
        P("group"),
        P("group"),
    )
    return jax.shard_map(
        shards,
        mesh=mesh,
        in_specs=placed,
        out_specs=(P(("group", "dp"), None, "tensor"), P(("group", "dp"), None)),
        check_vma=False,
    )
```

time: 277 us -> 135 us (0.49)
  Pallas kernels: 0 us -> 120 us
  matrix products: 96.5 us -> 0 us
  waiting for transfers between devices: 78.2 us -> 0 us
  other arithmetic: 42.6 us -> 3.55 us
  local copies, waits for them, and re-layouts: 47.8 us -> 10.1 us
  starting transfers between devices: 7.39 us -> 0 us
    pallas_call x0 -> x2, Pallas kernels: none -> 120 us  [the longest x1 115 us: shards(): pl.pallas_call(functools.partial(score_kernel, n, rows, slot_len), out_sh...]
    dot_general x9 -> x0, matrix products: 96.5 us -> none  [the longest x2 28.7 us: attend_block(): jnp.einsum('bshgp,phd->bshgd', prompt_probs, cache_pairs[:, :, 1], prefer...]
    all_to_all x1 -> x0, waiting for transfers between devices: 78.2 us -> none  [shards(): lax.all_to_all(pack_rows(local_rows, send_source, send_present), 'dp', sp...]
    reduce_sum x7 -> x5, other arithmetic: 29.6 us -> 1.36 us  [the longest x1 0.72 us: shards(): source_lens = jnp.sum(jnp.where(arriving, lens, 0), axis=0)]
    convert_element_type x6 -> x0, local copies, waits for them, and re-layouts: 15.5 us -> none  [the longest x4 9.13 us: attend_block(): return result.reshape(blocks, slot_len, feature_width).astype(jnp.bfloat16)]
    gather x2 -> x0, local copies, waits for them, and re-layouts: 9.99 us -> none  [the longest x1 5.01 us: shards(): attention = jnp.take(moved_rows, recv_pos, axis=0)]
    select_n x5 -> x1, other arithmetic: 9.9 us -> 0.1 us  [plan(): jnp.where(position[None, :] < lens[:, None], (k // per_block * rows + fir...]
    dot_general x3 -> x0, local copies, waits for them, and re-layouts: 7.54 us -> none  [the longest x2 7.47 us: attend_block(): jnp.einsum('bshgd,bthd->bshgt', query_split, own_pairs[:, :, :, 0], prefe...]
  transfers between devices with their start and end apart: 1 -> 0, of which waited for: 1 -> 0; matrix products, arithmetic and copies ran while one was open for 5% -> 0% of each run, Pallas kernels for 0% -> 0%
where the time goes in v1:
time: 135 us
  Pallas kernels  120 us (89%)
  local copies, waits for them, and re-layouts  10.1 us (7%)
  other arithmetic  3.55 us (3%)
    pallas_call x1, Pallas kernels, shards(): pl.pallas_call(functools.partial(score_kernel, n, rows, slot_len), out_sh...  115 us
    unnamed x8, local copies, waits for them, and re-layouts  6.08 us
    pallas_call x1, Pallas kernels, shards(): pl.pallas_call(functools.partial(place_kernel, rows, slot_len), out_shape...  5.18 us

profile of v1, /device:TPU:0, one launch (start us, length us, event | category | flops | bytes accessed | tf_op | source)
XLA Modules:
  0.0 134.6 jit_solution(11563762422875477997)
XLA Ops:
  0.6 0.7 dynamic-slice_bitcast_fusion
  1.3 0.7 fusion.3
  2.0 0.2 select_reduce_fusion.2
  2.2 0.7 fusion.2
  2.9 0.1 select_reduce_fusion
  3.1 0.1 add.151
  3.1 0.1 add.152
  3.2 0.1 add.153
  3.3 0.7 select_reduce_fusion.8
  4.0 0.2 select_reduce_fusion.6
  4.2 0.7 multiply_add_fusion
  4.9 0.1 select_reduce_fusion.4
  5.1 0.1 add.141
  5.1 0.1 add.142
  5.2 0.1 add.143
  5.3 0.1 add.145
  5.5 0.1 reduce_sum.128
  5.5 0.1 broadcast_in_dim.121
  5.6 0.1 broadcast_in_dim.122
  5.7 0.1 add_select_fusion
  5.8 0.1 select_n.82.tok_ref
  5.9 0.8 copy.27
  6.7 0.1 reshape.221.old_ref
  6.8 0.7 reshape.220.w_ref
  7.5 0.0 copy-start.1
  7.5 1.2 copy-done.1
  8.7 0.0 copy-start.2
  8.7 1.2 copy-done.2
  10.0 115.1 %shard_map.86 = (bf16[8,128,2048]{2,1,0:T(8,128)(2,1)}, f32[1,1024]{1,0:T(1,128)S(1)}) custom-call(s32[128]{0:T(128)S(1)} %get-tuple-element.18.order_ref, s32[8,1,128]{2,1,0:T(1,128)S(1)} %bitcast.28, s32[8,1,128]{2,1,0:T(1,128)S(1)} %bitcast.29, s32[1,1024]{1,0:T(1,128)S(1)} %select_n.82.tok_ref, bf16[128,8,2048]{2,1,0:T(8,128)(2,1)} %q_ref.1, ...), custom_call_target="tpu_custom_call" | custom-call | tf_op jit(solution)/shard_map/pallas_call | solution.py:237
  125.1 0.1 reduce_sum.121
  125.1 0.1 broadcast_in_dim.116
  125.2 0.1 broadcast_in_dim.117
  125.3 0.0 copy-start
  125.3 2.2 %copy-done = bf16[8,128,2048]{2,1,0:T(8,128)(2,1)S(1)} copy-done((bf16[8,128,2048]{2,1,0:T(8,128)(2,1)S(1)}, bf16[8,128,2048]{2,1,0:T(8,128)(2,1)}, u32[]{:S(2)}) %copy-start) | copy-done | bytes 4194328
  127.5 5.2 %shard_map.87 = bf16[128,8,2048]{2,1,0:T(8,128)(2,1)} custom-call(s32[128]{0:T(128)S(1)} %get-tuple-element.23.order_ref, s32[8,1,128]{2,1,0:T(1,128)S(1)} %bitcast.26, s32[8,1,128]{2,1,0:T(1,128)S(1)} %bitcast.27, bf16[8,128,2048]{2,1,0:T(8,128)(2,1)S(1)} %copy-done), custom_call_target="tpu_custom_call" | custom-call | tf_op jit(solution)/shard_map/pallas_call | solution.py:266
  132.7 0.5 broadcast.205
  133.2 0.7 reduce.3
  133.9 0.1 reshape.222
  134.0 0.7 copy.30
  (5 shorter events, 0.0 us)
Async XLA Ops:
  7.5 1.2 copy-start.1
  8.7 1.2 copy-start.2
  125.3 2.2 %copy-start = (bf16[8,128,2048]{2,1,0:T(8,128)(2,1)S(1)}, bf16[8,128,2048]{2,1,0:T(8,128)(2,1)}, u32[]{:S(2)}) copy-start(bf16[8,128,2048]{2,1,0:T(8,128)(2,1)} %get-tuple-element.4.recv_ref) | copy-start | bytes 12582916
